TPU v7x, 32 devices: a whole 2x2x4 slice. The times are simulated.
32 devices in a mesh: row: 4 (over z), col: 8 (over y, x, core).
Axes of the slice: x: 2, y: 2, z: 4, core: 2. Of those that a mesh axis runs over, the one named last changes fastest.
Arguments:
- gate_pre: bfloat16 [1024, 16384], P('row', 'col'), may hold values from -8 to 8
- up_pre: bfloat16 [1024, 16384], P('row', 'col'), may hold values from -6 to 6
- down_t: bfloat16 [4096, 16384], P('row', 'col'), may hold values from -0.09375 to 0.09375
- grad_out: bfloat16 [1024, 4096], P('row', 'col'), may hold values from -6 to 6
Outputs:
- gate_grad: bfloat16 [1024, 16384], P('row', 'col')
- up_grad: bfloat16 [1024, 16384], P('row', 'col')
- weight_grad: bfloat16 [4096, 16384], P('row', 'col')
All inputs are finite; a program needn't handle non-finite values.
Results may differ from a plain program's by a relative error of at most 0.0049.
Values may be sent and summed in bfloat16 or wider, within the bound.
No kernel may reach another device: no remote copies, remote signals or barrier semaphores. Data moves between devices by JAX's collectives and lax.ppermute only.
A program may use at most 128 MiB of HBM per device.

v0:
```python
import jax
import jax.numpy as jnp
from jax import lax
from jax.experimental import pallas as pl
from jax.experimental.pallas import tpu as pltpu
from jax.sharding import PartitionSpec as P

PARTS = 2


def after(value, first):
    return lax.optimization_barrier((value, first))[0]


def lay_strips(near, far):
    chips, rows, strip, width = near.shape

    def kernel(near_ref, far_ref, out_ref):
        row, col = lax.axis_index("row"), lax.axis_index("col")
        for core, ref in enumerate((near_ref, far_ref)):
            for chip in range(chips):
                owner = col ^ (2 * chip + core)
                for group in range(rows):
                    slot = lax.rem((row ^ group) + rows - row, rows)
                    start = pl.multiple_of((slot * 2 * chips + owner) * strip, strip)
                    out_ref[pl.ds(start, strip), :] = ref[chip, group]

    return pl.pallas_call(
        kernel,
        out_shape=jax.ShapeDtypeStruct((rows * 2 * chips * strip, width), near.dtype),
        in_specs=[pl.BlockSpec(memory_space=pltpu.VMEM)] * 2,
        out_specs=pl.BlockSpec(memory_space=pltpu.VMEM),
        compiler_params=pltpu.CompilerParams(vmem_limit_bytes=32 * 2**20),
        name="lay_strips",
    )(near, far)


def swap(value, bits):
    return lax.ppermute(value, "col", [(at, at ^ bits) for at in range(lax.axis_size("col"))])


def spread_cotangent(grad_out, hidden, first):
    rows, cols = lax.axis_size("row"), lax.axis_size("col")
    row = lax.axis_index("row")
    tok_rows, width = grad_out.shape
    per_row = cols // rows
    if (rows, cols) != (4, 8):
        pairs = [
            (src * cols + per_row * dst + part, dst * cols + per_row * ((src - dst) % rows) + part)
            for src in range(rows)
            for dst in range(rows)
            for part in range(per_row)
        ]
        moved = lax.ppermute(grad_out, ("row", "col"), pairs)
        blocks = lax.all_gather(moved, "col", axis=0)
        blocks = blocks.reshape(rows, per_row, tok_rows, width)
        return blocks.transpose(0, 2, 1, 3).reshape(rows * tok_rows, per_row * width)
    wide = after(lax.all_to_all(grad_out, "col", 0, 1, tiled=True), hidden)

    def across(bits):
        piece = lax.dynamic_slice_in_dim(wide, (row ^ bits) * per_row * width, per_row * width, 1)
        if bits == 0:
            return piece
        return lax.ppermute(piece, "row", [(at, at ^ bits) for at in range(rows)])

    tall = [across(bits) for bits in range(rows - 1, -1, -1)]
    tall = jnp.stack(tall[::-1])
    near = jnp.stack([tall, swap(tall, 2), swap(tall, 4), swap(tall, 6)])
    return lay_strips(*after((near, swap(near, 1)), first))


def per_device(gate_pre, up_pre, down_t, grad_out):
    rows = lax.axis_size("row")
    row = lax.axis_index("row")
    tok_rows, width = gate_pre.shape
    norm_scale = (tok_rows * rows) ** (-0.5)
    wire = jnp.bfloat16 if rows <= 4 else jnp.float32
    ahead = [(at, at + 1) for at in range(rows - 1)]
    behind = [(at + 1, at) for at in range(rows - 1)]
    span = tok_rows // PARTS

    def halves(value):
        return [value[at * span : (at + 1) * span] for at in range(PARTS)]

    gate_value = gate_pre.astype(jnp.float32)
    activated = gate_value * jax.nn.sigmoid(gate_value)
    hidden = (activated * up_pre.astype(jnp.float32)).astype(jnp.bfloat16)
    fore = [None, [lax.ppermute(hidden.astype(wire), "row", ahead)] * PARTS]
    back = [None, [lax.ppermute(hidden.astype(wire), "row", behind)] * PARTS]

    cot = spread_cotangent(grad_out, hidden, (fore[1][0], back[1][0]))
    turn = hidden
    for step in range(2, rows + 1):
        fore.append([None] * PARTS)
        back.append([None] * PARTS)
        cot_now = after(cot, turn)
        for at in range(PARTS):
            for way, (ends, slot, mine, pairs) in enumerate(
                ((fore, rows + 1 - step, step > row + 1, ahead), (back, step - 1, step > rows - row, behind))
            ):
                got = after(ends[step - 1][at], turn)
                if step == 2:
                    got = halves(got)[at]
                start = slot * tok_rows + at * span
                share = jnp.dot(cot_now[start : start + span], down_t, preferred_element_type=jnp.float32)
                total = got.astype(jnp.float32) + jnp.where(mine, share, 0.0)
                turn = total.astype(wire)
                ends[step][at] = lax.ppermute(turn, "row", pairs)
        late = turn

    pieces = [after(hidden, turn)]
    for slot in range(1, rows):
        for at in range(PARTS):
            ends = [back[slot][at], fore[rows - slot][at]]
            ends = [got if got.shape[0] == span else halves(got)[at] for got in ends]
            pieces.append(jnp.where(row + slot < rows, *ends).astype(jnp.bfloat16))
    weight_sum = lax.dot_general(
        cot,
        jnp.concatenate(pieces, axis=0),
        (((0,), (0,)), ((), ())),
        preferred_element_type=jnp.float32,
    )
    weight_grad = (weight_sum * norm_scale).astype(jnp.bfloat16)

    own_share = jnp.dot(after(cot[:tok_rows], late), down_t, preferred_element_type=jnp.float32)
    own_share, gate_again, up_again = after((own_share, gate_pre, up_pre), turn)
    gate_grad = up_grad = jnp.zeros((tok_rows, width), jnp.bfloat16)
    for at in range(PARTS):
        share, gate_cut, up_cut = (halves(value)[at] for value in (own_share, gate_again, up_again))
        hidden_grad = share + fore[rows][at].astype(jnp.float32) + back[rows][at].astype(jnp.float32)
        gate_cut = gate_cut.astype(jnp.float32)
        gate_sigmoid = jax.nn.sigmoid(gate_cut)
        up_part = (hidden_grad * (gate_cut * gate_sigmoid)).astype(jnp.bfloat16)
        slope = gate_sigmoid * (1.0 + gate_cut * (1.0 - gate_sigmoid))
        gate_part = (hidden_grad * up_cut.astype(jnp.float32) * slope).astype(jnp.bfloat16)
        gate_grad = lax.dynamic_update_slice(gate_grad, gate_part, (at * span, 0))
        up_grad = lax.dynamic_update_slice(up_grad, up_part, (at * span, 0))
        if at < PARTS - 1:
            gate_grad, up_grad = lax.optimization_barrier((gate_grad, up_grad))
    return gate_grad, up_grad, weight_grad


def solution(mesh):
    specs = (P("row", "col"),) * 4
    return jax.shard_map(
        per_device, mesh=mesh, in_specs=specs, out_specs=specs[:3], check_vma=False
    )
```

profile of v0, /device:TPU:0, one launch (start us, length us, event | category | flops | bytes accessed | tf_op | source)
XLA Modules:
  0.0 132.5 jit_solution(14875838950253225933)
XLA Ops:
  0.6 5.2 %all-to-all-start = ((bf16[8,32,512]{2,1,0:T(8,128)(2,1)}), bf16[8,32,512]{2,1,0:T(8,128)(2,1)S(1)}, u32[]{:S(2)}, u32[]{:S(2)}) async-start(bf16[8,32,512]{2,1,0:T(8,128)(2,1)} %bitcast.30), calls=%async_computation | async-start | bytes 524288 | tf_op jit(solution)/shard_map/all_to_all | solution.py:58
  5.8 2.2 %fusion.4 = bf16[256,2048]{1,0:T(8,128)(2,1)S(1)} fusion(bf16[256,2048]{1,0:T(8,128)(2,1)} %param.5, bf16[256,2048]{1,0:T(8,128)(2,1)} %param.4), kind=kLoop, calls=%fused_computation.15 | loop fusion | flops 4194304 | bytes 3145728 | tf_op jit(solution)/shard_map/convert_element_type | solution.py:87
  8.0 4.7 %all-to-all-done = bf16[8,32,512]{2,1,0:T(8,128)(2,1)S(1)} async-done(((bf16[8,32,512]{2,1,0:T(8,128)(2,1)}), bf16[8,32,512]{2,1,0:T(8,128)(2,1)S(1)}, u32[]{:S(2)}, u32[]{:S(2)}) %all-to-all-start) | async-done | bytes 262176 | tf_op jit(solution)/shard_map/all_to_all | solution.py:58
  14.5 2.6 %collective-permute-start.1 = (bf16[32,1024]{1,0:T(8,128)(2,1)S(1)}, bf16[32,1024]{1,0:T(8,128)(2,1)S(1)}, u32[]{:S(2)}, u32[]{:S(2)}) collective-permute-start(bf16[32,1024]{1,0:T(8,128)(2,1)S(1)} %get-tuple-element.61), channel_id=1, source_target_pairs={{0,16},{8,24},{16,0},{24,8},{1,17},{9,25},{17,1},{25,9},{2,18},{10... | collective-permute-start | bytes 196616 | tf_op jit(solution)/shard_map/ppermute | solution.py:64
  17.8 3.3 %collective-permute-done.1 = bf16[32,1024]{1,0:T(8,128)(2,1)S(1)} collective-permute-done((bf16[32,1024]{1,0:T(8,128)(2,1)S(1)}, bf16[32,1024]{1,0:T(8,128)(2,1)S(1)}, u32[]{:S(2)}, u32[]{:S(2)}) %collective-permute-start.1) | collective-permute-done | bytes 65568 | tf_op jit(solution)/shard_map/ppermute | solution.py:64
  21.1 2.0 %collective-permute-done.2 = bf16[32,1024]{1,0:T(8,128)(2,1)S(1)} collective-permute-done((bf16[32,1024]{1,0:T(8,128)(2,1)S(1)}, bf16[32,1024]{1,0:T(8,128)(2,1)S(1)}, u32[]{:S(2)}, u32[]{:S(2)}) %collective-permute-start.2) | collective-permute-done | bytes 65568 | tf_op jit(solution)/shard_map/ppermute | solution.py:64
  24.3 2.4 %collective-permute-start.5 = (bf16[4,32,1024]{2,1,0:T(8,128)(2,1)S(1)}, bf16[4,32,1024]{2,1,0:T(8,128)(2,1)S(1)}, u32[]{:S(2)}, u32[]{:S(2)}) collective-permute-start(bf16[4,32,1024]{2,1,0:T(8,128)(2,1)S(1)} %get-tuple-element.58), channel_id=1, source_target_pairs={{0,6},{1,7},{2,4},{3,5},{4,2},{5,3},{6,0},{7,1},{8,14},{9,15},{10,... | collective-permute-start | bytes 786440 | tf_op jit(solution)/shard_map/ppermute | solution.py:39
  26.7 2.3 %collective-permute-start.7 = (bf16[256,2048]{1,0:T(8,128)(2,1)S(1)}, bf16[256,2048]{1,0:T(8,128)(2,1)}, u32[]{:S(2)}, u32[]{:S(2)}) collective-permute-start(bf16[256,2048]{1,0:T(8,128)(2,1)S(1)} %fusion.4), channel_id=1, source_target_pairs={{0,8},{8,16},{16,24},{1,9},{9,17},{17,25},{2,10},{10,18},{18,26},{... | collective-permute-start | bytes 3145736 | tf_op jit(solution)/shard_map/ppermute | solution.py:88
  31.7 3.9 %collective-permute-done.4 = bf16[4,32,1024]{2,1,0:T(8,128)(2,1)S(1)} collective-permute-done((bf16[4,32,1024]{2,1,0:T(8,128)(2,1)S(1)}, bf16[4,32,1024]{2,1,0:T(8,128)(2,1)S(1)}, u32[]{:S(2)}, u32[]{:S(2)}) %collective-permute-start.4) | collective-permute-done | bytes 262176 | tf_op jit(solution)/shard_map/ppermute | solution.py:39
  35.9 12.4 %collective-permute-done.7 = bf16[256,2048]{1,0:T(8,128)(2,1)} collective-permute-done((bf16[256,2048]{1,0:T(8,128)(2,1)S(1)}, bf16[256,2048]{1,0:T(8,128)(2,1)}, u32[]{:S(2)}, u32[]{:S(2)}) %collective-permute-start.7) | collective-permute-done | bytes 1048608 | tf_op jit(solution)/shard_map/ppermute | solution.py:88
  48.3 5.2 %collective-permute-done.8 = bf16[256,2048]{1,0:T(8,128)(2,1)} collective-permute-done((bf16[256,2048]{1,0:T(8,128)(2,1)S(1)}, bf16[256,2048]{1,0:T(8,128)(2,1)}, u32[]{:S(2)}, u32[]{:S(2)}) %collective-permute-start.8) | collective-permute-done | bytes 1048608 | tf_op jit(solution)/shard_map/ppermute | solution.py:89
  53.7 2.2 %add_convert_fusion.11 = bf16[128,2048]{1,0:T(8,128)(2,1)S(1)} fusion(bf16[256,2048]{1,0:T(8,128)(2,1)} %collective-permute-done.7, bf16[1024,2048]{1,0:T(8,128)(2,1)S(1)} %copy-done.2, pred[]{:T(512)S(6)} %lt.50, bf16[1024,1024]{1,0:T(8,128)(2,1)S(1)} %lay_strips.1), kind=kOutput, calls=%fused_computation.54 | convolution fusion | flops 537919488 | bytes 5505025 | tf_op jit(solution)/shard_map/dot_general | solution.py:105
  55.9 2.8 %collective-permute-start.12 = (bf16[128,2048]{1,0:T(8,128)(2,1)S(1)}, bf16[128,2048]{1,0:T(8,128)(2,1)S(1)}, u32[]{:S(2)}, u32[]{:S(2)}) collective-permute-start(bf16[128,2048]{1,0:T(8,128)(2,1)S(1)} %add_convert_fusion.11), channel_id=1, source_target_pairs={{0,8},{8,16},{16,24},{1,9},{9,17},{17,25},{2,10},{10,18},{18,26},{... | collective-permute-start | bytes 1572872 | tf_op jit(solution)/shard_map/ppermute | solution.py:108
  61.7 1.8 %add_convert_fusion.9 = bf16[128,2048]{1,0:T(8,128)(2,1)S(1)} fusion(bf16[256,2048]{1,0:T(8,128)(2,1)} %collective-permute-done.7, bf16[1024,2048]{1,0:T(8,128)(2,1)S(1)} %copy-done.2, pred[]{:T(512)S(6)} %lt.50, bf16[1024,1024]{1,0:T(8,128)(2,1)S(1)} %lay_strips.1), kind=kOutput, calls=%fused_computation.52 | convolution fusion | flops 537919488 | bytes 5505025 | tf_op jit(solution)/shard_map/dot_general | solution.py:105
  63.5 4.6 %collective-permute-start.10 = (bf16[128,2048]{1,0:T(8,128)(2,1)S(1)}, bf16[128,2048]{1,0:T(8,128)(2,1)S(1)}, u32[]{:S(2)}, u32[]{:S(2)}) collective-permute-start(bf16[128,2048]{1,0:T(8,128)(2,1)S(1)} %add_convert_fusion.9), channel_id=1, source_target_pairs={{0,8},{8,16},{16,24},{1,9},{9,17},{17,25},{2,10},{10,18},{18,26},{... | collective-permute-start | bytes 1572872 | tf_op jit(solution)/shard_map/ppermute | solution.py:108
  72.8 4.6 %collective-permute-start.16 = (bf16[128,2048]{1,0:T(8,128)(2,1)S(1)}, bf16[128,2048]{1,0:T(8,128)(2,1)S(1)}, u32[]{:S(2)}, u32[]{:S(2)}) collective-permute-start(bf16[128,2048]{1,0:T(8,128)(2,1)S(1)} %add_convert_fusion.7), channel_id=1, source_target_pairs={{0,8},{8,16},{16,24},{1,9},{9,17},{17,25},{2,10},{10,18},{18,26},{... | collective-permute-start | bytes 1572872 | tf_op jit(solution)/shard_map/ppermute | solution.py:108
  80.6 4.4 %collective-permute-start.14 = (bf16[128,2048]{1,0:T(8,128)(2,1)S(1)}, bf16[128,2048]{1,0:T(8,128)(2,1)S(1)}, u32[]{:S(2)}, u32[]{:S(2)}) collective-permute-start(bf16[128,2048]{1,0:T(8,128)(2,1)S(1)} %add_convert_fusion.5), channel_id=1, source_target_pairs={{0,8},{8,16},{16,24},{1,9},{9,17},{17,25},{2,10},{10,18},{18,26},{... | collective-permute-start | bytes 1572872 | tf_op jit(solution)/shard_map/ppermute | solution.py:108
  85.0 3.1 %collective-permute-done.9 = bf16[128,2048]{1,0:T(8,128)(2,1)S(1)} collective-permute-done((bf16[128,2048]{1,0:T(8,128)(2,1)S(1)}, bf16[128,2048]{1,0:T(8,128)(2,1)S(1)}, u32[]{:S(2)}, u32[]{:S(2)}) %collective-permute-start.9) | collective-permute-done | bytes 524320 | tf_op jit(solution)/shard_map/ppermute | solution.py:108
  92.6 4.7 %collective-permute-start.17 = (bf16[128,2048]{1,0:T(8,128)(2,1)S(1)}, bf16[128,2048]{1,0:T(8,128)(2,1)S(1)}, u32[]{:S(2)}, u32[]{:S(2)}) collective-permute-start(bf16[128,2048]{1,0:T(8,128)(2,1)S(1)} %add_convert_fusion.3), channel_id=1, source_target_pairs={{0,8},{8,16},{16,24},{1,9},{9,17},{17,25},{2,10},{10,18},{18,26},{... | collective-permute-start | bytes 1572872 | tf_op jit(solution)/shard_map/ppermute | solution.py:108
  97.3 2.0 %collective-permute-done.15 = bf16[128,2048]{1,0:T(8,128)(2,1)S(1)} collective-permute-done((bf16[128,2048]{1,0:T(8,128)(2,1)S(1)}, bf16[128,2048]{1,0:T(8,128)(2,1)S(1)}, u32[]{:S(2)}, u32[]{:S(2)}) %collective-permute-start.15) | collective-permute-done | bytes 524320 | tf_op jit(solution)/shard_map/ppermute | solution.py:108
  100.8 2.2 %collective-permute-done.14 = bf16[128,2048]{1,0:T(8,128)(2,1)S(1)} collective-permute-done((bf16[128,2048]{1,0:T(8,128)(2,1)S(1)}, bf16[128,2048]{1,0:T(8,128)(2,1)S(1)}, u32[]{:S(2)}, u32[]{:S(2)}) %collective-permute-start.14) | collective-permute-done | bytes 524320 | tf_op jit(solution)/shard_map/ppermute | solution.py:108
  103.0 7.5 %collective-permute-done.13 = bf16[128,2048]{1,0:T(8,128)(2,1)S(1)} collective-permute-done((bf16[128,2048]{1,0:T(8,128)(2,1)S(1)}, bf16[128,2048]{1,0:T(8,128)(2,1)S(1)}, u32[]{:S(2)}, u32[]{:S(2)}) %collective-permute-start.13) | collective-permute-done | bytes 524320 | tf_op jit(solution)/shard_map/ppermute | solution.py:108
  112.0 4.8 %collective-permute-start.19 = (bf16[128,2048]{1,0:T(8,128)(2,1)S(1)}, bf16[128,2048]{1,0:T(8,128)(2,1)S(1)}, u32[]{:S(2)}, u32[]{:S(2)}) collective-permute-start(bf16[128,2048]{1,0:T(8,128)(2,1)S(1)} %add_convert_fusion.1), channel_id=1, source_target_pairs={{0,8},{8,16},{16,24},{1,9},{9,17},{17,25},{2,10},{10,18},{18,26},{... | collective-permute-start | bytes 1572872 | tf_op jit(solution)/shard_map/ppermute | solution.py:108
  123.3 6.2 %multiply_convert_fusion = bf16[1024,2048]{1,0:T(8,128)(2,1)} fusion(bf16[1024,1024]{1,0:T(8,128)(2,1)S(1)} %copy-done.1, bf16[1024,2048]{1,0:T(8,128)(2,1)S(1)} %fusion.23), kind=kOutput, calls=%fused_computation | convolution fusion | flops 4299161600 | bytes 10485760 | tf_op jit(solution)/shard_map/dot_general | solution.py:117
  (73 shorter events, 34.4 us)
Async XLA Ops:
  0.6 12.1 %all-to-all-start = ((bf16[8,32,512]{2,1,0:T(8,128)(2,1)}), bf16[8,32,512]{2,1,0:T(8,128)(2,1)S(1)}, u32[]{:S(2)}, u32[]{:S(2)}) async-start(bf16[8,32,512]{2,1,0:T(8,128)(2,1)} %bitcast.30), calls=%async_computation | async-start | bytes 524288 | tf_op jit(solution)/shard_map/all_to_all | solution.py:58
  12.8 5.0 %collective-permute-start = (bf16[32,1024]{1,0:T(8,128)(2,1)S(1)}, bf16[32,1024]{1,0:T(8,128)(2,1)S(1)}, u32[]{:S(2)}, u32[]{:S(2)}) collective-permute-start(bf16[32,1024]{1,0:T(8,128)(2,1)S(1)} %get-tuple-element.62), channel_id=1, source_target_pairs={{0,8},{8,0},{16,24},{24,16},{1,9},{9,1},{17,25},{25,17},{2,10},{10... | collective-permute-start | bytes 196616 | tf_op jit(solution)/shard_map/ppermute | solution.py:64
  14.5 6.6 %collective-permute-start.1 = (bf16[32,1024]{1,0:T(8,128)(2,1)S(1)}, bf16[32,1024]{1,0:T(8,128)(2,1)S(1)}, u32[]{:S(2)}, u32[]{:S(2)}) collective-permute-start(bf16[32,1024]{1,0:T(8,128)(2,1)S(1)} %get-tuple-element.61), channel_id=1, source_target_pairs={{0,16},{8,24},{16,0},{24,8},{1,17},{9,25},{17,1},{25,9},{2,18},{10... | collective-permute-start | bytes 196616 | tf_op jit(solution)/shard_map/ppermute | solution.py:64
  17.0 6.1 %collective-permute-start.2 = (bf16[32,1024]{1,0:T(8,128)(2,1)S(1)}, bf16[32,1024]{1,0:T(8,128)(2,1)S(1)}, u32[]{:S(2)}, u32[]{:S(2)}) collective-permute-start(bf16[32,1024]{1,0:T(8,128)(2,1)S(1)} %get-tuple-element.60), channel_id=1, source_target_pairs={{0,24},{8,16},{16,8},{24,0},{1,25},{9,17},{17,9},{25,1},{2,26},{10... | collective-permute-start | bytes 196616 | tf_op jit(solution)/shard_map/ppermute | solution.py:64
  23.2 8.6 %collective-permute-start.3 = (bf16[4,32,1024]{2,1,0:T(8,128)(2,1)S(1)}, bf16[4,32,1024]{2,1,0:T(8,128)(2,1)S(1)}, u32[]{:S(2)}, u32[]{:S(2)}) collective-permute-start(bf16[4,32,1024]{2,1,0:T(8,128)(2,1)S(1)} %get-tuple-element.58), channel_id=1, source_target_pairs={{0,2},{1,3},{2,0},{3,1},{4,6},{5,7},{6,4},{7,5},{8,10},{9,11},{10,... | collective-permute-start | bytes 786440 | tf_op jit(solution)/shard_map/ppermute | solution.py:39
  23.9 11.8 %collective-permute-start.4 = (bf16[4,32,1024]{2,1,0:T(8,128)(2,1)S(1)}, bf16[4,32,1024]{2,1,0:T(8,128)(2,1)S(1)}, u32[]{:S(2)}, u32[]{:S(2)}) collective-permute-start(bf16[4,32,1024]{2,1,0:T(8,128)(2,1)S(1)} %get-tuple-element.58), channel_id=1, source_target_pairs={{0,4},{1,5},{2,6},{3,7},{4,0},{5,1},{6,2},{7,3},{8,12},{9,13},{10,... | collective-permute-start | bytes 786440 | tf_op jit(solution)/shard_map/ppermute | solution.py:39
  24.3 11.3 %collective-permute-start.5 = (bf16[4,32,1024]{2,1,0:T(8,128)(2,1)S(1)}, bf16[4,32,1024]{2,1,0:T(8,128)(2,1)S(1)}, u32[]{:S(2)}, u32[]{:S(2)}) collective-permute-start(bf16[4,32,1024]{2,1,0:T(8,128)(2,1)S(1)} %get-tuple-element.58), channel_id=1, source_target_pairs={{0,6},{1,7},{2,4},{3,5},{4,2},{5,3},{6,0},{7,1},{8,14},{9,15},{10,... | collective-permute-start | bytes 786440 | tf_op jit(solution)/shard_map/ppermute | solution.py:39
  26.7 21.6 %collective-permute-start.7 = (bf16[256,2048]{1,0:T(8,128)(2,1)S(1)}, bf16[256,2048]{1,0:T(8,128)(2,1)}, u32[]{:S(2)}, u32[]{:S(2)}) collective-permute-start(bf16[256,2048]{1,0:T(8,128)(2,1)S(1)} %fusion.4), channel_id=1, source_target_pairs={{0,8},{8,16},{16,24},{1,9},{9,17},{17,25},{2,10},{10,18},{18,26},{... | collective-permute-start | bytes 3145736 | tf_op jit(solution)/shard_map/ppermute | solution.py:88
  29.0 24.5 %collective-permute-start.8 = (bf16[256,2048]{1,0:T(8,128)(2,1)S(1)}, bf16[256,2048]{1,0:T(8,128)(2,1)}, u32[]{:S(2)}, u32[]{:S(2)}) collective-permute-start(bf16[256,2048]{1,0:T(8,128)(2,1)S(1)} %fusion.4), channel_id=1, source_target_pairs={{8,0},{16,8},{24,16},{9,1},{17,9},{25,17},{10,2},{18,10},{26,18},{... | collective-permute-start | bytes 3145736 | tf_op jit(solution)/shard_map/ppermute | solution.py:89
  35.8 17.7 %collective-permute-start.6 = (bf16[4,4,32,1024]{3,2,1,0:T(8,128)(2,1)S(1)}, bf16[4,4,32,1024]{3,2,1,0:T(8,128)(2,1)S(1)}, u32[]{:S(2)}, u32[]{:S(2)}) collective-permute-start(bf16[4,4,32,1024]{3,2,1,0:T(8,128)(2,1)S(1)} %pad_maximum_fusion.near_ref), channel_id=1, source_target_pairs={{0,1},{1,0},{2,3},{3,2},{4,5},{5,4},{6,7},{7,6},{8,9},{9,8},{10,11... | collective-permute-start | bytes 3145736 | tf_op jit(solution)/shard_map/ppermute | solution.py:39
  53.7 38.0 %copy-start = (bf16[1024,1024]{1,0:T(8,128)(2,1)}, bf16[1024,1024]{1,0:T(8,128)(2,1)S(1)}, u32[]{:S(2)}) copy-start(bf16[1024,1024]{1,0:T(8,128)(2,1)S(1)} %lay_strips.1) | copy-start | bytes 6291460
  55.9 16.8 %collective-permute-start.12 = (bf16[128,2048]{1,0:T(8,128)(2,1)S(1)}, bf16[128,2048]{1,0:T(8,128)(2,1)S(1)}, u32[]{:S(2)}, u32[]{:S(2)}) collective-permute-start(bf16[128,2048]{1,0:T(8,128)(2,1)S(1)} %add_convert_fusion.11), channel_id=1, source_target_pairs={{0,8},{8,16},{16,24},{1,9},{9,17},{17,25},{2,10},{10,18},{18,26},{... | collective-permute-start | bytes 1572872 | tf_op jit(solution)/shard_map/ppermute | solution.py:108
  60.4 16.9 %collective-permute-start.11 = (bf16[128,2048]{1,0:T(8,128)(2,1)S(1)}, bf16[128,2048]{1,0:T(8,128)(2,1)S(1)}, u32[]{:S(2)}, u32[]{:S(2)}) collective-permute-start(bf16[128,2048]{1,0:T(8,128)(2,1)S(1)} %add_convert_fusion.10), channel_id=1, source_target_pairs={{8,0},{16,8},{24,16},{9,1},{17,9},{25,17},{10,2},{18,10},{26,18},{... | collective-permute-start | bytes 1572872 | tf_op jit(solution)/shard_map/ppermute | solution.py:108
  63.5 16.9 %collective-permute-start.10 = (bf16[128,2048]{1,0:T(8,128)(2,1)S(1)}, bf16[128,2048]{1,0:T(8,128)(2,1)S(1)}, u32[]{:S(2)}, u32[]{:S(2)}) collective-permute-start(bf16[128,2048]{1,0:T(8,128)(2,1)S(1)} %add_convert_fusion.9), channel_id=1, source_target_pairs={{0,8},{8,16},{16,24},{1,9},{9,17},{17,25},{2,10},{10,18},{18,26},{... | collective-permute-start | bytes 1572872 | tf_op jit(solution)/shard_map/ppermute | solution.py:108
  71.4 16.8 %collective-permute-start.9 = (bf16[128,2048]{1,0:T(8,128)(2,1)S(1)}, bf16[128,2048]{1,0:T(8,128)(2,1)S(1)}, u32[]{:S(2)}, u32[]{:S(2)}) collective-permute-start(bf16[128,2048]{1,0:T(8,128)(2,1)S(1)} %add_convert_fusion.8), channel_id=1, source_target_pairs={{8,0},{16,8},{24,16},{9,1},{17,9},{25,17},{10,2},{18,10},{26,18},{... | collective-permute-start | bytes 1572872 | tf_op jit(solution)/shard_map/ppermute | solution.py:108
  72.8 19.7 %collective-permute-start.16 = (bf16[128,2048]{1,0:T(8,128)(2,1)S(1)}, bf16[128,2048]{1,0:T(8,128)(2,1)S(1)}, u32[]{:S(2)}, u32[]{:S(2)}) collective-permute-start(bf16[128,2048]{1,0:T(8,128)(2,1)S(1)} %add_convert_fusion.7), channel_id=1, source_target_pairs={{0,8},{8,16},{16,24},{1,9},{9,17},{17,25},{2,10},{10,18},{18,26},{... | collective-permute-start | bytes 1572872 | tf_op jit(solution)/shard_map/ppermute | solution.py:108
  77.5 21.8 %collective-permute-start.15 = (bf16[128,2048]{1,0:T(8,128)(2,1)S(1)}, bf16[128,2048]{1,0:T(8,128)(2,1)S(1)}, u32[]{:S(2)}, u32[]{:S(2)}) collective-permute-start(bf16[128,2048]{1,0:T(8,128)(2,1)S(1)} %add_convert_fusion.6), channel_id=1, source_target_pairs={{8,0},{16,8},{24,16},{9,1},{17,9},{25,17},{10,2},{18,10},{26,18},{... | collective-permute-start | bytes 1572872 | tf_op jit(solution)/shard_map/ppermute | solution.py:108
  80.6 22.3 %collective-permute-start.14 = (bf16[128,2048]{1,0:T(8,128)(2,1)S(1)}, bf16[128,2048]{1,0:T(8,128)(2,1)S(1)}, u32[]{:S(2)}, u32[]{:S(2)}) collective-permute-start(bf16[128,2048]{1,0:T(8,128)(2,1)S(1)} %add_convert_fusion.5), channel_id=1, source_target_pairs={{0,8},{8,16},{16,24},{1,9},{9,17},{17,25},{2,10},{10,18},{18,26},{... | collective-permute-start | bytes 1572872 | tf_op jit(solution)/shard_map/ppermute | solution.py:108
  89.7 20.9 %collective-permute-start.13 = (bf16[128,2048]{1,0:T(8,128)(2,1)S(1)}, bf16[128,2048]{1,0:T(8,128)(2,1)S(1)}, u32[]{:S(2)}, u32[]{:S(2)}) collective-permute-start(bf16[128,2048]{1,0:T(8,128)(2,1)S(1)} %add_convert_fusion.4), channel_id=1, source_target_pairs={{8,0},{16,8},{24,16},{9,1},{17,9},{25,17},{10,2},{18,10},{26,18},{... | collective-permute-start | bytes 1572872 | tf_op jit(solution)/shard_map/ppermute | solution.py:108
  92.6 24.2 %slice-start = ((bf16[1024,1024]{1,0:T(8,128)(2,1)}), bf16[256,1024]{1,0:T(8,128)(2,1)S(1)}, s32[]{:S(2)}) async-start(bf16[1024,1024]{1,0:T(8,128)(2,1)} %copy-done), calls=%async_computation.1 | async-start | bytes 1048576 | tf_op jit(solution)/shard_map/slice | solution.py:125
  92.6 36.9 %collective-permute-start.17 = (bf16[128,2048]{1,0:T(8,128)(2,1)S(1)}, bf16[128,2048]{1,0:T(8,128)(2,1)S(1)}, u32[]{:S(2)}, u32[]{:S(2)}) collective-permute-start(bf16[128,2048]{1,0:T(8,128)(2,1)S(1)} %add_convert_fusion.3), channel_id=1, source_target_pairs={{0,8},{8,16},{16,24},{1,9},{9,17},{17,25},{2,10},{10,18},{18,26},{... | collective-permute-start | bytes 1572872 | tf_op jit(solution)/shard_map/ppermute | solution.py:108
  99.5 30.1 %collective-permute-start.18 = (bf16[128,2048]{1,0:T(8,128)(2,1)S(1)}, bf16[128,2048]{1,0:T(8,128)(2,1)S(1)}, u32[]{:S(2)}, u32[]{:S(2)}) collective-permute-start(bf16[128,2048]{1,0:T(8,128)(2,1)S(1)} %add_convert_fusion.2), channel_id=1, source_target_pairs={{8,0},{16,8},{24,16},{9,1},{17,9},{25,17},{10,2},{18,10},{26,18},{... | collective-permute-start | bytes 1572872 | tf_op jit(solution)/shard_map/ppermute | solution.py:108
  110.7 19.8 %collective-permute-start.20 = (bf16[128,2048]{1,0:T(8,128)(2,1)S(1)}, bf16[128,2048]{1,0:T(8,128)(2,1)S(1)}, u32[]{:S(2)}, u32[]{:S(2)}) collective-permute-start(bf16[128,2048]{1,0:T(8,128)(2,1)S(1)} %add_convert_fusion), channel_id=1, source_target_pairs={{8,0},{16,8},{24,16},{9,1},{17,9},{25,17},{10,2},{18,10},{26,18},{... | collective-permute-start | bytes 1572872 | tf_op jit(solution)/shard_map/ppermute | solution.py:108
  112.0 18.5 %collective-permute-start.19 = (bf16[128,2048]{1,0:T(8,128)(2,1)S(1)}, bf16[128,2048]{1,0:T(8,128)(2,1)S(1)}, u32[]{:S(2)}, u32[]{:S(2)}) collective-permute-start(bf16[128,2048]{1,0:T(8,128)(2,1)S(1)} %add_convert_fusion.1), channel_id=1, source_target_pairs={{0,8},{8,16},{16,24},{1,9},{9,17},{17,25},{2,10},{10,18},{18,26},{... | collective-permute-start | bytes 1572872 | tf_op jit(solution)/shard_map/ppermute | solution.py:108
  (6 other events, 36.5 us)
where the time goes:
time: 133 us; the launch traced here: 132 us
  starting transfers between devices  50.4 us (38%)
  waiting for transfers between devices  50 us (38%)
  matrix products  19.3 us (15%)
  other arithmetic  9.87 us (7%)
  local copies, waits for them, and re-layouts  1.66 us (1%)
    ppermute x12, starting transfers between devices, per_device(): ends[step][at] = lax.ppermute(turn, 'row', pairs)  33.6 us
    ppermute x12, waiting for transfers between devices, per_device(): ends[step][at] = lax.ppermute(turn, 'row', pairs)  16.4 us
    ppermute x1, waiting for transfers between devices, per_device(): fore = [None, [lax.ppermute(hidden.astype(wire), 'row', ahead)] * PARTS]  12.4 us
    dot_general x10, matrix products, per_device(): jnp.dot(cot_now[start:start + span], down_t, preferred_element_type=jnp.f...  11.8 us
    dot_general x1, matrix products, per_device(): lax.dot_general(cot, jnp.concatenate(pieces, axis=0), (((0,), (0,)), ((),...  6.2 us
    ppermute x3, waiting for transfers between devices, across(): return lax.ppermute(piece, 'row', [(at, at ^ bits) for at in range(rows)])  5.84 us
    ppermute x4, waiting for transfers between devices, swap(): lax.ppermute(value, 'col', [(at, at ^ bits) for at in range(lax.axis_size...  5.38 us
    ppermute x1, waiting for transfers between devices, per_device(): back = [None, [lax.ppermute(hidden.astype(wire), 'row', behind)] * PARTS]  5.19 us
  transfers between devices with their start and end apart: 22, of which 13 were waited for; matrix products, arithmetic and copies ran while one was open for 20% of the time, Pallas kernels for 0%

commit v1 on v0

v1 whole, which is shorter than its diff:
```python
import jax
import jax.numpy as jnp
from jax import lax
from jax.experimental import pallas as pl
from jax.experimental.pallas import tpu as pltpu
from jax.sharding import PartitionSpec as P

PARTS = 2


def after(value, first):
    return lax.optimization_barrier((value, first))[0]


def lay_strips(near, far):
    chips, rows, strip, width = near.shape

    def kernel(near_ref, far_ref, out_ref):
        row, col = lax.axis_index("row"), lax.axis_index("col")
        for at, ref in enumerate((near_ref, far_ref)):
            lane = pl.multiple_of(((col & 1) ^ at) * width, width)
            for chip in range(chips):
                for group in range(rows):
                    slot = lax.rem((row ^ group) + rows - row, rows)
                    start = (slot * chips + (col // 2 ^ chip)) * strip
                    out_ref[pl.ds(pl.multiple_of(start, strip), strip), pl.ds(lane, width)] = ref[chip, group]

    return pl.pallas_call(
        kernel,
        out_shape=jax.ShapeDtypeStruct((rows * chips * strip, 2 * width), near.dtype),
        in_specs=[pl.BlockSpec(memory_space=pltpu.VMEM)] * 2,
        out_specs=pl.BlockSpec(memory_space=pltpu.VMEM),
        compiler_params=pltpu.CompilerParams(vmem_limit_bytes=32 * 2**20),
        name="lay_strips",
    )(near, far)


def add_share(got, cot, down_t, start, mine):
    span, width = got.shape
    tile = 512 if width % 512 == 0 else width

    def kernel(got_ref, cot_ref, down_ref, out_ref):
        is_sum = mine(lax.axis_index("row"))

        @pl.when(is_sum)
        def _():
            tokens = cot_ref[start : start + span, :]
            for at in range(0, width, tile):
                share = jnp.dot(tokens, down_ref[:, at : at + tile], preferred_element_type=jnp.float32)
                total = got_ref[:, at : at + tile].astype(jnp.float32) + share
                out_ref[:, at : at + tile] = total.astype(out_ref.dtype)

        @pl.when(jnp.logical_not(is_sum))
        def _():
            out_ref[...] = got_ref[...]

    whole = pl.BlockSpec(memory_space=pltpu.VMEM)
    return pl.pallas_call(
        kernel,
        out_shape=jax.ShapeDtypeStruct(got.shape, got.dtype),
        in_specs=[whole] * 3,
        out_specs=whole,
        compiler_params=pltpu.CompilerParams(vmem_limit_bytes=32 * 2**20),
        cost_estimate=pl.CostEstimate(
            flops=2 * span * down_t.size, bytes_accessed=2 * got.nbytes, transcendentals=0
        ),
        name="add_share",
    )(got, cot, down_t)


def weight_product(cot, own, fore, back, scale):
    rows, parts = len(fore) + 1, len(fore[0])
    tok_rows, width = own.shape
    span = tok_rows // parts
    tile = 512 if width % 512 == 0 else width
    flat = [piece for pieces in fore + back for piece in pieces]

    def kernel(cot_ref, own_ref, *refs):
        ends, out_ref, hidden_ref = refs[: len(flat)], refs[len(flat)], refs[len(flat) + 1]
        row = lax.axis_index("row")

        def place(end, start, cut):
            rows_here = pl.ds(start, end.shape[0])
            hidden_ref[rows_here, :] = end[:, cut].astype(hidden_ref.dtype)

        @pl.loop(0, width // tile)
        def _(at):
            cut = pl.ds(pl.multiple_of(at * tile, tile), tile)
            hidden_ref[:tok_rows, :] = own_ref[:, cut]
            for slot in range(1, rows):
                for part in range(parts):
                    ahead = ends[(rows - slot - 1) * parts + part]
                    behind = ends[(rows - 1 + slot - 1) * parts + part]
                    start = slot * tok_rows + part * span
                    pl.when(row + slot < rows)(lambda end=behind, start=start: place(end, start, cut))
                    pl.when(row + slot >= rows)(lambda end=ahead, start=start: place(end, start, cut))
            total = lax.dot_general(
                cot_ref[...],
                hidden_ref[...],
                (((0,), (0,)), ((), ())),
                preferred_element_type=jnp.float32,
            )
            out_ref[:, cut] = (total * scale).astype(out_ref.dtype)

    whole = pl.BlockSpec(memory_space=pltpu.VMEM)
    return pl.pallas_call(
        kernel,
        out_shape=jax.ShapeDtypeStruct((cot.shape[1], width), jnp.bfloat16),
        in_specs=[whole] * (2 + len(flat)),
        out_specs=whole,
        scratch_shapes=[pltpu.VMEM((cot.shape[0], tile), jnp.bfloat16)],
        compiler_params=pltpu.CompilerParams(vmem_limit_bytes=32 * 2**20),
        cost_estimate=pl.CostEstimate(
            flops=2 * cot.size * width, bytes_accessed=4 * cot.shape[0] * width, transcendentals=0
        ),
        name="weight_product",
    )(cot, own, *flat)


def swap(value, bits):
    return lax.ppermute(value, "col", [(at, at ^ bits) for at in range(lax.axis_size("col"))])


def spread_cotangent(grad_out, hidden, first):
    rows, cols = lax.axis_size("row"), lax.axis_size("col")
    row = lax.axis_index("row")
    tok_rows, width = grad_out.shape
    per_row = cols // rows
    if (rows, cols) != (4, 8):
        pairs = [
            (src * cols + per_row * dst + part, dst * cols + per_row * ((src - dst) % rows) + part)
            for src in range(rows)
            for dst in range(rows)
            for part in range(per_row)
        ]
        moved = lax.ppermute(grad_out, ("row", "col"), pairs)
        blocks = lax.all_gather(moved, "col", axis=0)
        blocks = blocks.reshape(rows, per_row, tok_rows, width)
        return blocks.transpose(0, 2, 1, 3).reshape(rows * tok_rows, per_row * width)
    strip = tok_rows * 2 // cols
    chip = lax.axis_index("col") // 2

    def quarter(bits):
        piece = lax.dynamic_slice_in_dim(grad_out, (chip ^ bits) * strip, strip, 0)
        return swap(piece, 2 * bits) if bits else piece

    wide = after([quarter(bits) for bits in range(cols // 2)], hidden[0])

    def across(bits):
        piece = lax.dynamic_index_in_dim(jnp.stack(wide), chip ^ row ^ bits, 0, keepdims=False)
        return lax.ppermute(piece, "row", [(at, at ^ bits) for at in range(rows)]) if bits else piece

    tall = [across(bits) for bits in range(rows - 1, -1, -1)]
    tall = jnp.stack(tall[::-1])
    near = jnp.stack([tall, swap(tall, 2), swap(tall, 4), swap(tall, 6)])
    near = after(near, first)
    return lay_strips(near, swap(near, 1))


def per_device(gate_pre, up_pre, down_t, grad_out):
    rows = lax.axis_size("row")
    row = lax.axis_index("row")
    tok_rows, width = gate_pre.shape
    norm_scale = (tok_rows * rows) ** (-0.5)
    wire = jnp.bfloat16 if rows <= 4 else jnp.float32
    ahead = [(at, at + 1) for at in range(rows - 1)]
    behind = [(at + 1, at) for at in range(rows - 1)]
    span = tok_rows // PARTS

    def halves(value):
        return [value[at * span : (at + 1) * span] for at in range(PARTS)]

    hidden, fore, back = [], [None, []], [None, []]
    for gate_cut, up_cut in zip(halves(gate_pre), halves(up_pre)):
        gate_cut = gate_cut.astype(jnp.float32)
        activated = gate_cut * jax.nn.sigmoid(gate_cut)
        hidden.append((activated * up_cut.astype(jnp.float32)).astype(jnp.bfloat16))
        fore[1].append(lax.ppermute(hidden[-1].astype(wire), "row", ahead))
        back[1].append(lax.ppermute(hidden[-1].astype(wire), "row", behind))

    cot = spread_cotangent(grad_out, hidden, (fore[1][0], back[1][0]))
    turn = hidden[0]
    for step in range(2, rows + 1):
        fore.append([None] * PARTS)
        back.append([None] * PARTS)
        for at in range(PARTS):
            for ends, slot, mine, pairs in (
                (fore, rows + 1 - step, lambda row, step=step: step > row + 1, ahead),
                (back, step - 1, lambda row, step=step: step > rows - row, behind),
            ):
                got = after(ends[step - 1][at], turn)
                turn = add_share(got, cot, down_t, slot * tok_rows + at * span, mine)
                ends[step][at] = lax.ppermute(turn, "row", pairs)
        late = turn

    weight_grad = weight_product(cot, jnp.concatenate(hidden), fore[1:rows], back[1:rows], norm_scale)

    own_share = jnp.dot(after(cot[:tok_rows], late), down_t, preferred_element_type=jnp.float32)
    own_share, gate_again, up_again = after((own_share, gate_pre, up_pre), turn)
    gate_grad = up_grad = jnp.zeros((tok_rows, width), jnp.bfloat16)
    for at in range(PARTS):
        share, gate_cut, up_cut = (halves(value)[at] for value in (own_share, gate_again, up_again))
        hidden_grad = share + fore[rows][at].astype(jnp.float32) + back[rows][at].astype(jnp.float32)
        gate_cut = gate_cut.astype(jnp.float32)
        gate_sigmoid = jax.nn.sigmoid(gate_cut)
        up_part = (hidden_grad * (gate_cut * gate_sigmoid)).astype(jnp.bfloat16)
        slope = gate_sigmoid * (1.0 + gate_cut * (1.0 - gate_sigmoid))
        gate_part = (hidden_grad * up_cut.astype(jnp.float32) * slope).astype(jnp.bfloat16)
        gate_grad = lax.dynamic_update_slice(gate_grad, gate_part, (at * span, 0))
        up_grad = lax.dynamic_update_slice(up_grad, up_part, (at * span, 0))
        if at < PARTS - 1:
            gate_grad, up_grad = lax.optimization_barrier((gate_grad, up_grad))
    return gate_grad, up_grad, weight_grad


def solution(mesh):
    specs = (P("row", "col"),) * 4
    return jax.shard_map(
        per_device, mesh=mesh, in_specs=specs, out_specs=specs[:3], check_vma=False
    )
```

time: 133 us -> 122 us (0.917)
  matrix products: 19.3 us -> 1.24 us
  Pallas kernels: 0.15 us -> 12.4 us
  other arithmetic: 9.87 us -> 3.81 us
  waiting for transfers between devices: 50 us -> 44.7 us
  starting transfers between devices: 50.4 us -> 55.6 us
    ppermute x5 -> x7, waiting for transfers between devices: 23.5 us -> 5.4 us  [the longest x2 4.68 us: per_device(): fore[1].append(lax.ppermute(hidden[-1].astype(wire), 'row', ahead))]
    dot_general x11 -> x0, matrix products: 18 us -> none  [the longest x10 11.8 us: per_device(): jnp.dot(cot_now[start:start + span], down_t, preferred_element_type=jnp.f...]
    ppermute x12, waiting for transfers between devices: 16.4 us -> 29.1 us  [per_device(): ends[step][at] = lax.ppermute(turn, 'row', pairs)]
    pallas_call x1 -> x14, Pallas kernels: 0.15 us -> 12.4 us  [the longest x1 7.58 us: weight_product(): pl.pallas_call(kernel, out_shape=jax.ShapeDtypeStruct((cot.shape[1], widt...]
    ppermute x5 -> x7, starting transfers between devices: 8 us -> 14.2 us  [the longest x2 7.21 us: per_device(): fore[1].append(lax.ppermute(hidden[-1].astype(wire), 'row', ahead))]
    all_to_all x1 -> x0, starting transfers between devices: 5.18 us -> none  [spread_cotangent(): wide = after(lax.all_to_all(grad_out, 'col', 0, 1, tiled=True), hidden)]
    ppermute x4 -> x7, waiting for transfers between devices: 5.38 us -> 10.2 us  [swap(): lax.ppermute(value, 'col', [(at, at ^ bits) for at in range(lax.axis_size...]
    all_to_all x1 -> x0, waiting for transfers between devices: 4.7 us -> none  [spread_cotangent(): wide = after(lax.all_to_all(grad_out, 'col', 0, 1, tiled=True), hidden)]
  transfers between devices with their start and end apart: 22 -> 26, of which waited for: 13 -> 12; matrix products, arithmetic and copies ran while one was open for 20% -> 4% of each run, Pallas kernels for 0% -> 10%
where the time goes in v1:
time: 122 us
  starting transfers between devices  55.6 us (46%)
  waiting for transfers between devices  44.7 us (37%)
  Pallas kernels  12.4 us (10%)
  other arithmetic  3.81 us (3%)
  local copies, waits for them, and re-layouts  2.55 us (2%)
  matrix products  1.24 us (1%)
    ppermute x12, starting transfers between devices, per_device(): ends[step][at] = lax.ppermute(turn, 'row', pairs)  33.2 us
    ppermute x12, waiting for transfers between devices, per_device(): ends[step][at] = lax.ppermute(turn, 'row', pairs)  29.1 us
    ppermute x7, waiting for transfers between devices, swap(): lax.ppermute(value, 'col', [(at, at ^ bits) for at in range(lax.axis_size...  10.2 us
    ppermute x7, starting transfers between devices, swap(): lax.ppermute(value, 'col', [(at, at ^ bits) for at in range(lax.axis_size...  8.17 us
    pallas_call x1, Pallas kernels, weight_product(): pl.pallas_call(kernel, out_shape=jax.ShapeDtypeStruct((cot.shape[1], widt...  7.58 us
    ppermute x2, starting transfers between devices, per_device(): fore[1].append(lax.ppermute(hidden[-1].astype(wire), 'row', ahead))  7.21 us
    ppermute x2, waiting for transfers between devices, per_device(): fore[1].append(lax.ppermute(hidden[-1].astype(wire), 'row', ahead))  4.68 us
    pallas_call x12, Pallas kernels, add_share(): pl.pallas_call(kernel, out_shape=jax.ShapeDtypeStruct(got.shape, got.dtyp...  4.68 us
  transfers between devices with their start and end apart: 26, of which 12 were waited for; matrix products, arithmetic and copies ran while one was open for 4% of the time, Pallas kernels for 10%

profile of v1, /device:TPU:0, one launch (start us, length us, event | category | flops | bytes accessed | tf_op | source)
XLA Modules:
  0.0 121.5 jit_solution(2697857108969246952)
XLA Ops:
  1.6 3.0 %collective-permute-start = (bf16[64,512]{1,0:T(8,128)(2,1)S(1)}, bf16[64,512]{1,0:T(8,128)(2,1)S(1)}, u32[]{:S(2)}, u32[]{:S(2)}) collective-permute-start(bf16[64,512]{1,0:T(8,128)(2,1)S(1)} %get-tuple-element.62), channel_id=1, source_target_pairs={{0,2},{1,3},{2,0},{3,1},{4,6},{5,7},{6,4},{7,5},{8,10},{9,11},{10,... | collective-permute-start | bytes 196616 | tf_op jit(solution)/shard_map/ppermute | solution.py:121
  4.6 1.5 %collective-permute-start.1 = (bf16[64,512]{1,0:T(8,128)(2,1)S(1)}, bf16[64,512]{1,0:T(8,128)(2,1)S(1)}, u32[]{:S(2)}, u32[]{:S(2)}) collective-permute-start(bf16[64,512]{1,0:T(8,128)(2,1)S(1)} %get-tuple-element.64), channel_id=1, source_target_pairs={{0,4},{1,5},{2,6},{3,7},{4,0},{5,1},{6,2},{7,3},{8,12},{9,13},{10,... | collective-permute-start | bytes 196616 | tf_op jit(solution)/shard_map/ppermute | solution.py:121
  6.2 2.2 %fusion.26 = (bf16[128,2048]{1,0:T(8,128)(2,1)S(1)}, bf16[128,2048]{1,0:T(8,128)(2,1)S(1)}) fusion(bf16[256,2048]{1,0:T(8,128)(2,1)} %param.5, bf16[256,2048]{1,0:T(8,128)(2,1)} %param.4), kind=kLoop, calls=%fused_computation.40 | loop fusion | flops 4194304 | bytes 3145728 | tf_op jit(solution)/shard_map/convert_element_type | solution.py:177
  8.9 2.4 %collective-permute-done.2 = bf16[64,512]{1,0:T(8,128)(2,1)S(1)} collective-permute-done((bf16[64,512]{1,0:T(8,128)(2,1)S(1)}, bf16[64,512]{1,0:T(8,128)(2,1)S(1)}, u32[]{:S(2)}, u32[]{:S(2)}) %collective-permute-start.2) | collective-permute-done | bytes 65568 | tf_op jit(solution)/shard_map/ppermute | solution.py:121
  11.4 1.6 %collective-permute-start.3 = (bf16[64,512]{1,0:T(8,128)(2,1)S(1)}, bf16[64,512]{1,0:T(8,128)(2,1)S(1)}, u32[]{:S(2)}, u32[]{:S(2)}) collective-permute-start(bf16[64,512]{1,0:T(8,128)(2,1)S(1)} %get-tuple-element.60), channel_id=1, source_target_pairs={{0,8},{8,0},{16,24},{24,16},{1,9},{9,1},{17,25},{25,17},{2,10},{10... | collective-permute-start | bytes 196616 | tf_op jit(solution)/shard_map/ppermute | solution.py:151
  13.0 2.6 %collective-permute-start.4 = (bf16[64,512]{1,0:T(8,128)(2,1)S(1)}, bf16[64,512]{1,0:T(8,128)(2,1)S(1)}, u32[]{:S(2)}, u32[]{:S(2)}) collective-permute-start(bf16[64,512]{1,0:T(8,128)(2,1)S(1)} %get-tuple-element.59), channel_id=1, source_target_pairs={{0,16},{8,24},{16,0},{24,8},{1,17},{9,25},{17,1},{25,9},{2,18},{10... | collective-permute-start | bytes 196616 | tf_op jit(solution)/shard_map/ppermute | solution.py:151
  17.1 4.6 %collective-permute-start.9 = (bf16[128,2048]{1,0:T(8,128)(2,1)S(1)}, bf16[128,2048]{1,0:T(8,128)(2,1)S(1)}, u32[]{:S(2)}, u32[]{:S(2)}) collective-permute-start(bf16[128,2048]{1,0:T(8,128)(2,1)S(1)} %get-tuple-element.54), channel_id=1, source_target_pairs={{0,8},{8,16},{16,24},{1,9},{9,17},{17,25},{2,10},{10,18},{18,26},{... | collective-permute-start | bytes 1572872 | tf_op jit(solution)/shard_map/ppermute | solution.py:178
  23.6 2.4 %collective-permute-start.8 = (bf16[4,64,512]{2,1,0:T(8,128)(2,1)S(1)}, bf16[4,64,512]{2,1,0:T(8,128)(2,1)S(1)}, u32[]{:S(2)}, u32[]{:S(2)}) collective-permute-start(bf16[4,64,512]{2,1,0:T(8,128)(2,1)S(1)} %get-tuple-element.56), channel_id=1, source_target_pairs={{0,6},{1,7},{2,4},{3,5},{4,2},{5,3},{6,0},{7,1},{8,14},{9,15},{10,... | collective-permute-start | bytes 786440 | tf_op jit(solution)/shard_map/ppermute | solution.py:121
  26.1 3.8 %collective-permute-done.6 = bf16[4,64,512]{2,1,0:T(8,128)(2,1)S(1)} collective-permute-done((bf16[4,64,512]{2,1,0:T(8,128)(2,1)S(1)}, bf16[4,64,512]{2,1,0:T(8,128)(2,1)S(1)}, u32[]{:S(2)}, u32[]{:S(2)}) %collective-permute-start.6) | collective-permute-done | bytes 262176 | tf_op jit(solution)/shard_map/ppermute | solution.py:121
  29.9 3.4 %collective-permute-done.7 = bf16[4,64,512]{2,1,0:T(8,128)(2,1)S(1)} collective-permute-done((bf16[4,64,512]{2,1,0:T(8,128)(2,1)S(1)}, bf16[4,64,512]{2,1,0:T(8,128)(2,1)S(1)}, u32[]{:S(2)}, u32[]{:S(2)}) %collective-permute-start.7) | collective-permute-done | bytes 262176 | tf_op jit(solution)/shard_map/ppermute | solution.py:121
  33.6 2.6 %collective-permute-start.13 = (bf16[128,2048]{1,0:T(8,128)(2,1)S(1)}, bf16[128,2048]{1,0:T(8,128)(2,1)S(1)}, u32[]{:S(2)}, u32[]{:S(2)}) collective-permute-start(bf16[128,2048]{1,0:T(8,128)(2,1)S(1)} %get-tuple-element.53), channel_id=1, source_target_pairs={{0,8},{8,16},{16,24},{1,9},{9,17},{17,25},{2,10},{10,18},{18,26},{... | collective-permute-start | bytes 1572872 | tf_op jit(solution)/shard_map/ppermute | solution.py:178
  38.5 3.9 %collective-permute-start.17 = (bf16[128,2048]{1,0:T(8,128)(2,1)S(1)}, bf16[128,2048]{1,0:T(8,128)(2,1)S(1)}, u32[]{:S(2)}, u32[]{:S(2)}) collective-permute-start(bf16[128,2048]{1,0:T(8,128)(2,1)S(1)} %add_share.12), channel_id=1, source_target_pairs={{0,8},{8,16},{16,24},{1,9},{9,17},{17,25},{2,10},{10,18},{18,26},{... | collective-permute-start | bytes 1572872 | tf_op jit(solution)/shard_map/ppermute | solution.py:193
  43.7 4.7 %collective-permute-done.13.got_ref.refs_1_ = bf16[128,2048]{1,0:T(8,128)(2,1)S(1)} collective-permute-done((bf16[128,2048]{1,0:T(8,128)(2,1)S(1)}, bf16[128,2048]{1,0:T(8,128)(2,1)S(1)}, u32[]{:S(2)}, u32[]{:S(2)}) %collective-permute-start.13) | collective-permute-done | bytes 524320 | tf_op jit(solution)/shard_map/ppermute | solution.py:178
  49.1 3.7 %collective-permute-start.15 = (bf16[128,2048]{1,0:T(8,128)(2,1)S(1)}, bf16[128,2048]{1,0:T(8,128)(2,1)S(1)}, u32[]{:S(2)}, u32[]{:S(2)}) collective-permute-start(bf16[128,2048]{1,0:T(8,128)(2,1)S(1)} %add_share.14), channel_id=1, source_target_pairs={{0,8},{8,16},{16,24},{1,9},{9,17},{17,25},{2,10},{10,18},{18,26},{... | collective-permute-start | bytes 1572872 | tf_op jit(solution)/shard_map/ppermute | solution.py:193
  54.2 5.4 %collective-permute-done.17.got_ref.refs_2_ = bf16[128,2048]{1,0:T(8,128)(2,1)S(1)} collective-permute-done((bf16[128,2048]{1,0:T(8,128)(2,1)S(1)}, bf16[128,2048]{1,0:T(8,128)(2,1)S(1)}, u32[]{:S(2)}, u32[]{:S(2)}) %collective-permute-start.17) | collective-permute-done | bytes 524320 | tf_op jit(solution)/shard_map/ppermute | solution.py:193
  60.4 4.4 %collective-permute-start.21 = (bf16[128,2048]{1,0:T(8,128)(2,1)S(1)}, bf16[128,2048]{1,0:T(8,128)(2,1)S(1)}, u32[]{:S(2)}, u32[]{:S(2)}) collective-permute-start(bf16[128,2048]{1,0:T(8,128)(2,1)S(1)} %add_share.16), channel_id=1, source_target_pairs={{0,8},{8,16},{16,24},{1,9},{9,17},{17,25},{2,10},{10,18},{18,26},{... | collective-permute-start | bytes 1572872 | tf_op jit(solution)/shard_map/ppermute | solution.py:193
  66.2 4.7 %collective-permute-done.15.got_ref.refs_3_ = bf16[128,2048]{1,0:T(8,128)(2,1)S(1)} collective-permute-done((bf16[128,2048]{1,0:T(8,128)(2,1)S(1)}, bf16[128,2048]{1,0:T(8,128)(2,1)S(1)}, u32[]{:S(2)}, u32[]{:S(2)}) %collective-permute-start.15) | collective-permute-done | bytes 524320 | tf_op jit(solution)/shard_map/ppermute | solution.py:193
  71.6 4.4 %collective-permute-start.19 = (bf16[128,2048]{1,0:T(8,128)(2,1)S(1)}, bf16[128,2048]{1,0:T(8,128)(2,1)S(1)}, u32[]{:S(2)}, u32[]{:S(2)}) collective-permute-start(bf16[128,2048]{1,0:T(8,128)(2,1)S(1)} %add_share.18), channel_id=1, source_target_pairs={{0,8},{8,16},{16,24},{1,9},{9,17},{17,25},{2,10},{10,18},{18,26},{... | collective-permute-start | bytes 1572872 | tf_op jit(solution)/shard_map/ppermute | solution.py:193
  77.5 4.6 %collective-permute-done.21.got_ref.refs_4_ = bf16[128,2048]{1,0:T(8,128)(2,1)S(1)} collective-permute-done((bf16[128,2048]{1,0:T(8,128)(2,1)S(1)}, bf16[128,2048]{1,0:T(8,128)(2,1)S(1)}, u32[]{:S(2)}, u32[]{:S(2)}) %collective-permute-start.21) | collective-permute-done | bytes 524320 | tf_op jit(solution)/shard_map/ppermute | solution.py:193
  82.8 4.4 %collective-permute-start.22 = (bf16[128,2048]{1,0:T(8,128)(2,1)S(1)}, bf16[128,2048]{1,0:T(8,128)(2,1)S(1)}, u32[]{:S(2)}, u32[]{:S(2)}) collective-permute-start(bf16[128,2048]{1,0:T(8,128)(2,1)S(1)} %add_share.20), channel_id=1, source_target_pairs={{0,8},{8,16},{16,24},{1,9},{9,17},{17,25},{2,10},{10,18},{18,26},{... | collective-permute-start | bytes 1572872 | tf_op jit(solution)/shard_map/ppermute | solution.py:193
  88.6 4.7 %collective-permute-done.19.got_ref.refs_5_ = bf16[128,2048]{1,0:T(8,128)(2,1)S(1)} collective-permute-done((bf16[128,2048]{1,0:T(8,128)(2,1)S(1)}, bf16[128,2048]{1,0:T(8,128)(2,1)S(1)}, u32[]{:S(2)}, u32[]{:S(2)}) %collective-permute-start.19) | collective-permute-done | bytes 524320 | tf_op jit(solution)/shard_map/ppermute | solution.py:193
  94.1 4.4 %collective-permute-start.24 = (bf16[128,2048]{1,0:T(8,128)(2,1)S(1)}, bf16[128,2048]{1,0:T(8,128)(2,1)S(1)}, u32[]{:S(2)}, u32[]{:S(2)}) collective-permute-start(bf16[128,2048]{1,0:T(8,128)(2,1)S(1)} %add_share.22), channel_id=1, source_target_pairs={{0,8},{8,16},{16,24},{1,9},{9,17},{17,25},{2,10},{10,18},{18,26},{... | collective-permute-start | bytes 1572872 | tf_op jit(solution)/shard_map/ppermute | solution.py:193
  101.3 7.6 %weight_product.1 = bf16[1024,2048]{1,0:T(8,128)(2,1)} custom-call(bf16[1024,1024]{1,0:T(8,128)(2,1)S(1)} %lay_strips.1.cot_ref, bf16[256,2048]{1,0:T(8,128)(2,1)S(1)} %pad_maximum_fusion.1.own_ref, bf16[128,2048]{1,0:T(8,128)(2,1)S(1)} %collective-permute-done.9.got_ref.refs_0_, bf16[128,2048]{1,0:T(8,128)(2,1)S(1)} %collective-permute-done.13.got_ref.refs_1_, ...), custom_call_target="tpu_custom_call" | custom-call | flops 4294967296 | bytes 8388608 | tf_op jit(solution)/shard_map/weight_product/pallas_call | solution.py:106
  109.9 9.6 %collective-permute-done.25 = bf16[128,2048]{1,0:T(8,128)(2,1)S(1)} collective-permute-done((bf16[128,2048]{1,0:T(8,128)(2,1)S(1)}, bf16[128,2048]{1,0:T(8,128)(2,1)S(1)}, u32[]{:S(2)}, u32[]{:S(2)}) %collective-permute-start.25) | collective-permute-done | bytes 524320 | tf_op jit(solution)/shard_map/ppermute | solution.py:193
  (65 shorter events, 23.6 us)
Async XLA Ops:
  1.6 6.8 %collective-permute-start = (bf16[64,512]{1,0:T(8,128)(2,1)S(1)}, bf16[64,512]{1,0:T(8,128)(2,1)S(1)}, u32[]{:S(2)}, u32[]{:S(2)}) collective-permute-start(bf16[64,512]{1,0:T(8,128)(2,1)S(1)} %get-tuple-element.62), channel_id=1, source_target_pairs={{0,2},{1,3},{2,0},{3,1},{4,6},{5,7},{6,4},{7,5},{8,10},{9,11},{10,... | collective-permute-start | bytes 196616 | tf_op jit(solution)/shard_map/ppermute | solution.py:121
  6.2 5.2 %collective-permute-start.2 = (bf16[64,512]{1,0:T(8,128)(2,1)S(1)}, bf16[64,512]{1,0:T(8,128)(2,1)S(1)}, u32[]{:S(2)}, u32[]{:S(2)}) collective-permute-start(bf16[64,512]{1,0:T(8,128)(2,1)S(1)} %get-tuple-element.61), channel_id=1, source_target_pairs={{0,6},{1,7},{2,4},{3,5},{4,2},{5,3},{6,0},{7,1},{8,14},{9,15},{10,... | collective-permute-start | bytes 196616 | tf_op jit(solution)/shard_map/ppermute | solution.py:121
  11.4 10.3 %collective-permute-start.3 = (bf16[64,512]{1,0:T(8,128)(2,1)S(1)}, bf16[64,512]{1,0:T(8,128)(2,1)S(1)}, u32[]{:S(2)}, u32[]{:S(2)}) collective-permute-start(bf16[64,512]{1,0:T(8,128)(2,1)S(1)} %get-tuple-element.60), channel_id=1, source_target_pairs={{0,8},{8,0},{16,24},{24,16},{1,9},{9,1},{17,25},{25,17},{2,10},{10... | collective-permute-start | bytes 196616 | tf_op jit(solution)/shard_map/ppermute | solution.py:151
  13.0 8.7 %collective-permute-start.4 = (bf16[64,512]{1,0:T(8,128)(2,1)S(1)}, bf16[64,512]{1,0:T(8,128)(2,1)S(1)}, u32[]{:S(2)}, u32[]{:S(2)}) collective-permute-start(bf16[64,512]{1,0:T(8,128)(2,1)S(1)} %get-tuple-element.59), channel_id=1, source_target_pairs={{0,16},{8,24},{16,0},{24,8},{1,17},{9,25},{17,1},{25,9},{2,18},{10... | collective-permute-start | bytes 196616 | tf_op jit(solution)/shard_map/ppermute | solution.py:151
  15.6 6.8 %collective-permute-start.5 = (bf16[64,512]{1,0:T(8,128)(2,1)S(1)}, bf16[64,512]{1,0:T(8,128)(2,1)S(1)}, u32[]{:S(2)}, u32[]{:S(2)}) collective-permute-start(bf16[64,512]{1,0:T(8,128)(2,1)S(1)} %get-tuple-element.58), channel_id=1, source_target_pairs={{0,24},{8,16},{16,8},{24,0},{1,25},{9,17},{17,9},{25,1},{2,26},{10... | collective-permute-start | bytes 196616 | tf_op jit(solution)/shard_map/ppermute | solution.py:151
  15.9 17.6 %collective-permute-start.10 = (bf16[128,2048]{1,0:T(8,128)(2,1)S(1)}, bf16[128,2048]{1,0:T(8,128)(2,1)S(1)}, u32[]{:S(2)}, u32[]{:S(2)}) collective-permute-start(bf16[128,2048]{1,0:T(8,128)(2,1)S(1)} %get-tuple-element.54), channel_id=1, source_target_pairs={{8,0},{16,8},{24,16},{9,1},{17,9},{25,17},{10,2},{18,10},{26,18},{... | collective-permute-start | bytes 1572872 | tf_op jit(solution)/shard_map/ppermute | solution.py:179
  17.1 16.3 %collective-permute-start.9 = (bf16[128,2048]{1,0:T(8,128)(2,1)S(1)}, bf16[128,2048]{1,0:T(8,128)(2,1)S(1)}, u32[]{:S(2)}, u32[]{:S(2)}) collective-permute-start(bf16[128,2048]{1,0:T(8,128)(2,1)S(1)} %get-tuple-element.54), channel_id=1, source_target_pairs={{0,8},{8,16},{16,24},{1,9},{9,17},{17,25},{2,10},{10,18},{18,26},{... | collective-permute-start | bytes 1572872 | tf_op jit(solution)/shard_map/ppermute | solution.py:178
  22.5 7.4 %collective-permute-start.6 = (bf16[4,64,512]{2,1,0:T(8,128)(2,1)S(1)}, bf16[4,64,512]{2,1,0:T(8,128)(2,1)S(1)}, u32[]{:S(2)}, u32[]{:S(2)}) collective-permute-start(bf16[4,64,512]{2,1,0:T(8,128)(2,1)S(1)} %get-tuple-element.56), channel_id=1, source_target_pairs={{0,2},{1,3},{2,0},{3,1},{4,6},{5,7},{6,4},{7,5},{8,10},{9,11},{10,... | collective-permute-start | bytes 786440 | tf_op jit(solution)/shard_map/ppermute | solution.py:121
  23.1 10.2 %collective-permute-start.7 = (bf16[4,64,512]{2,1,0:T(8,128)(2,1)S(1)}, bf16[4,64,512]{2,1,0:T(8,128)(2,1)S(1)}, u32[]{:S(2)}, u32[]{:S(2)}) collective-permute-start(bf16[4,64,512]{2,1,0:T(8,128)(2,1)S(1)} %get-tuple-element.56), channel_id=1, source_target_pairs={{0,4},{1,5},{2,6},{3,7},{4,0},{5,1},{6,2},{7,3},{8,12},{9,13},{10,... | collective-permute-start | bytes 786440 | tf_op jit(solution)/shard_map/ppermute | solution.py:121
  23.6 9.7 %collective-permute-start.8 = (bf16[4,64,512]{2,1,0:T(8,128)(2,1)S(1)}, bf16[4,64,512]{2,1,0:T(8,128)(2,1)S(1)}, u32[]{:S(2)}, u32[]{:S(2)}) collective-permute-start(bf16[4,64,512]{2,1,0:T(8,128)(2,1)S(1)} %get-tuple-element.56), channel_id=1, source_target_pairs={{0,6},{1,7},{2,4},{3,5},{4,2},{5,3},{6,0},{7,1},{8,14},{9,15},{10,... | collective-permute-start | bytes 786440 | tf_op jit(solution)/shard_map/ppermute | solution.py:121
  33.6 14.8 %collective-permute-start.13 = (bf16[128,2048]{1,0:T(8,128)(2,1)S(1)}, bf16[128,2048]{1,0:T(8,128)(2,1)S(1)}, u32[]{:S(2)}, u32[]{:S(2)}) collective-permute-start(bf16[128,2048]{1,0:T(8,128)(2,1)S(1)} %get-tuple-element.53), channel_id=1, source_target_pairs={{0,8},{8,16},{16,24},{1,9},{9,17},{17,25},{2,10},{10,18},{18,26},{... | collective-permute-start | bytes 1572872 | tf_op jit(solution)/shard_map/ppermute | solution.py:178
  36.2 16.7 %collective-permute-start.12 = (bf16[128,2048]{1,0:T(8,128)(2,1)S(1)}, bf16[128,2048]{1,0:T(8,128)(2,1)S(1)}, u32[]{:S(2)}, u32[]{:S(2)}) collective-permute-start(bf16[128,2048]{1,0:T(8,128)(2,1)S(1)} %get-tuple-element.53), channel_id=1, source_target_pairs={{8,0},{16,8},{24,16},{9,1},{17,9},{25,17},{10,2},{18,10},{26,18},{... | collective-permute-start | bytes 1572872 | tf_op jit(solution)/shard_map/ppermute | solution.py:179
  38.5 21.2 %collective-permute-start.17 = (bf16[128,2048]{1,0:T(8,128)(2,1)S(1)}, bf16[128,2048]{1,0:T(8,128)(2,1)S(1)}, u32[]{:S(2)}, u32[]{:S(2)}) collective-permute-start(bf16[128,2048]{1,0:T(8,128)(2,1)S(1)} %add_share.12), channel_id=1, source_target_pairs={{0,8},{8,16},{16,24},{1,9},{9,17},{17,25},{2,10},{10,18},{18,26},{... | collective-permute-start | bytes 1572872 | tf_op jit(solution)/shard_map/ppermute | solution.py:193
  42.4 22.4 %collective-permute-start.16 = (bf16[128,2048]{1,0:T(8,128)(2,1)S(1)}, bf16[128,2048]{1,0:T(8,128)(2,1)S(1)}, u32[]{:S(2)}, u32[]{:S(2)}) collective-permute-start(bf16[128,2048]{1,0:T(8,128)(2,1)S(1)} %add_share.13), channel_id=1, source_target_pairs={{8,0},{16,8},{24,16},{9,1},{17,9},{25,17},{10,2},{18,10},{26,18},{... | collective-permute-start | bytes 1572872 | tf_op jit(solution)/shard_map/ppermute | solution.py:193
  49.1 21.7 %collective-permute-start.15 = (bf16[128,2048]{1,0:T(8,128)(2,1)S(1)}, bf16[128,2048]{1,0:T(8,128)(2,1)S(1)}, u32[]{:S(2)}, u32[]{:S(2)}) collective-permute-start(bf16[128,2048]{1,0:T(8,128)(2,1)S(1)} %add_share.14), channel_id=1, source_target_pairs={{0,8},{8,16},{16,24},{1,9},{9,17},{17,25},{2,10},{10,18},{18,26},{... | collective-permute-start | bytes 1572872 | tf_op jit(solution)/shard_map/ppermute | solution.py:193
  52.9 23.1 %collective-permute-start.14 = (bf16[128,2048]{1,0:T(8,128)(2,1)S(1)}, bf16[128,2048]{1,0:T(8,128)(2,1)S(1)}, u32[]{:S(2)}, u32[]{:S(2)}) collective-permute-start(bf16[128,2048]{1,0:T(8,128)(2,1)S(1)} %add_share.15), channel_id=1, source_target_pairs={{8,0},{16,8},{24,16},{9,1},{17,9},{25,17},{10,2},{18,10},{26,18},{... | collective-permute-start | bytes 1572872 | tf_op jit(solution)/shard_map/ppermute | solution.py:193
  60.4 21.7 %collective-permute-start.21 = (bf16[128,2048]{1,0:T(8,128)(2,1)S(1)}, bf16[128,2048]{1,0:T(8,128)(2,1)S(1)}, u32[]{:S(2)}, u32[]{:S(2)}) collective-permute-start(bf16[128,2048]{1,0:T(8,128)(2,1)S(1)} %add_share.16), channel_id=1, source_target_pairs={{0,8},{8,16},{16,24},{1,9},{9,17},{17,25},{2,10},{10,18},{18,26},{... | collective-permute-start | bytes 1572872 | tf_op jit(solution)/shard_map/ppermute | solution.py:193
  64.9 22.4 %collective-permute-start.20 = (bf16[128,2048]{1,0:T(8,128)(2,1)S(1)}, bf16[128,2048]{1,0:T(8,128)(2,1)S(1)}, u32[]{:S(2)}, u32[]{:S(2)}) collective-permute-start(bf16[128,2048]{1,0:T(8,128)(2,1)S(1)} %add_share.17), channel_id=1, source_target_pairs={{8,0},{16,8},{24,16},{9,1},{17,9},{25,17},{10,2},{18,10},{26,18},{... | collective-permute-start | bytes 1572872 | tf_op jit(solution)/shard_map/ppermute | solution.py:193
  71.6 21.7 %collective-permute-start.19 = (bf16[128,2048]{1,0:T(8,128)(2,1)S(1)}, bf16[128,2048]{1,0:T(8,128)(2,1)S(1)}, u32[]{:S(2)}, u32[]{:S(2)}) collective-permute-start(bf16[128,2048]{1,0:T(8,128)(2,1)S(1)} %add_share.18), channel_id=1, source_target_pairs={{0,8},{8,16},{16,24},{1,9},{9,17},{17,25},{2,10},{10,18},{18,26},{... | collective-permute-start | bytes 1572872 | tf_op jit(solution)/shard_map/ppermute | solution.py:193
  76.1 22.4 %collective-permute-start.18 = (bf16[128,2048]{1,0:T(8,128)(2,1)S(1)}, bf16[128,2048]{1,0:T(8,128)(2,1)S(1)}, u32[]{:S(2)}, u32[]{:S(2)}) collective-permute-start(bf16[128,2048]{1,0:T(8,128)(2,1)S(1)} %add_share.19), channel_id=1, source_target_pairs={{8,0},{16,8},{24,16},{9,1},{17,9},{25,17},{10,2},{18,10},{26,18},{... | collective-permute-start | bytes 1572872 | tf_op jit(solution)/shard_map/ppermute | solution.py:193
  82.8 26.2 %collective-permute-start.22 = (bf16[128,2048]{1,0:T(8,128)(2,1)S(1)}, bf16[128,2048]{1,0:T(8,128)(2,1)S(1)}, u32[]{:S(2)}, u32[]{:S(2)}) collective-permute-start(bf16[128,2048]{1,0:T(8,128)(2,1)S(1)} %add_share.20), channel_id=1, source_target_pairs={{0,8},{8,16},{16,24},{1,9},{9,17},{17,25},{2,10},{10,18},{18,26},{... | collective-permute-start | bytes 1572872 | tf_op jit(solution)/shard_map/ppermute | solution.py:193
  87.3 21.7 %collective-permute-start.23 = (bf16[128,2048]{1,0:T(8,128)(2,1)S(1)}, bf16[128,2048]{1,0:T(8,128)(2,1)S(1)}, u32[]{:S(2)}, u32[]{:S(2)}) collective-permute-start(bf16[128,2048]{1,0:T(8,128)(2,1)S(1)} %add_share.21), channel_id=1, source_target_pairs={{8,0},{16,8},{24,16},{9,1},{17,9},{25,17},{10,2},{18,10},{26,18},{... | collective-permute-start | bytes 1572872 | tf_op jit(solution)/shard_map/ppermute | solution.py:193
  94.1 25.5 %collective-permute-start.24 = (bf16[128,2048]{1,0:T(8,128)(2,1)S(1)}, bf16[128,2048]{1,0:T(8,128)(2,1)S(1)}, u32[]{:S(2)}, u32[]{:S(2)}) collective-permute-start(bf16[128,2048]{1,0:T(8,128)(2,1)S(1)} %add_share.22), channel_id=1, source_target_pairs={{0,8},{8,16},{16,24},{1,9},{9,17},{17,25},{2,10},{10,18},{18,26},{... | collective-permute-start | bytes 1572872 | tf_op jit(solution)/shard_map/ppermute | solution.py:193
  98.6 21.0 %collective-permute-start.25 = (bf16[128,2048]{1,0:T(8,128)(2,1)S(1)}, bf16[128,2048]{1,0:T(8,128)(2,1)S(1)}, u32[]{:S(2)}, u32[]{:S(2)}) collective-permute-start(bf16[128,2048]{1,0:T(8,128)(2,1)S(1)} %add_share.23), channel_id=1, source_target_pairs={{8,0},{16,8},{24,16},{9,1},{17,9},{25,17},{10,2},{18,10},{26,18},{... | collective-permute-start | bytes 1572872 | tf_op jit(solution)/shard_map/ppermute | solution.py:193
  (7 other events, 30.2 us)
